TPU v7x, 256 devices: a whole 4x4x8 slice. The times are simulated.
256 devices in a mesh: row: 8 (over x, core), col: 32 (over y, z).
Axes of the slice: x: 4, y: 4, z: 8, core: 2. Of those that a mesh axis runs over, the one named last changes fastest.
Arguments:
- tokens: bfloat16 [1024, 12288], P('col', 'row'), may hold values from -6 to 6
- weight: bfloat16 [12288, 49152], P('row', 'col'), may hold values from -0.0546875 to 0.0546875
- bias: float32 [49152], P('col'), may hold values from -3 to 3
- grad_hidden: bfloat16 [1024, 49152], P('row', 'col'), may hold values from -1.1953125 to 1.1953125
Outputs:
- hidden: bfloat16 [1024, 49152], P('row', 'col')
- grad_tokens: bfloat16 [1024, 12288], P('col', 'row')
- grad_weight: bfloat16 [12288, 49152], P('row', 'col')
- grad_bias: float32 [49152], P('col')
All inputs are finite; a program needn't handle non-finite values.
Results may differ from a plain program's by a relative error of at most 0.005.
Values may be sent and summed in bfloat16 or wider, within the bound.
A program may use at most 128 MiB of HBM per device.

v0:
```python
import math

import jax
import jax.numpy as jnp
from jax import lax
from jax.sharding import PartitionSpec as P

coeff = math.sqrt(2.0 / math.pi)


def gelu_value(z):
    inner = coeff * (z + 0.044715 * z * z * z)
    return 0.5 * z * (1.0 + jnp.tanh(inner))


def gelu_slope(z):
    inner = coeff * (z + 0.044715 * z * z * z)
    tval = jnp.tanh(inner)
    return 0.5 * (1.0 + tval) + 0.5 * z * (1.0 - tval * tval) * coeff * (
        1.0 + 3.0 * 0.044715 * z * z
    )


def body(tokens, weight, bias, grad_hidden):
    gathered = lax.all_gather(tokens, "col", axis=0, tiled=True)
    bias_row = bias[None, :]
    block = gathered
    preact = (
        lax.psum_scatter(
            jnp.dot(block, weight, preferred_element_type=jnp.float32),
            "row",
            scatter_dimension=0,
            tiled=True,
        )
        + bias_row
    )
    hidden = gelu_value(preact).astype(jnp.bfloat16)
    slope = (grad_hidden.astype(jnp.float32) * gelu_slope(preact)).astype(jnp.bfloat16)
    panel = lax.all_gather(slope, "row", axis=0, tiled=True)
    block = panel
    grad_tokens = lax.psum_scatter(
        lax.dot_general(
            block, weight, (((1,), (1,)), ((), ())), preferred_element_type=jnp.float32
        ),
        "col",
        scatter_dimension=0,
        tiled=True,
    ).astype(jnp.bfloat16)
    grad_weight = lax.dot_general(
        gathered, panel, (((0,), (0,)), ((), ())), preferred_element_type=jnp.float32
    ).astype(jnp.bfloat16)
    grad_bias = jnp.sum(panel.astype(jnp.float32), axis=0)
    return (hidden, grad_tokens, grad_weight, grad_bias)


def solution(mesh):
    in_specs = (P("col", "row"), P("row", "col"), P("col"), P("row", "col"))
    out_specs = (P("row", "col"), P("col", "row"), P("row", "col"), P("col"))
    return jax.shard_map(body, mesh=mesh, in_specs=in_specs, out_specs=out_specs, check_vma=False)
```

profile of v0, /device:TPU:33, one launch (start us, length us, event | category | flops | bytes accessed | tf_op | source)
XLA Modules:
  0.0 415.4 jit_solution(9864146275272268978)
XLA Ops:
  7.2 0.0 all-gather.3.cloned.1.call-start
  7.2 0.7 all-gather.3.cloned.1.call-update
  7.9 0.0 reduce-scatter.3.cloned.1.call-start
  7.9 81.2 %all-gather.3.cloned.1.call-done = bf16[1024,1536]{1,0:T(8,128)(2,1)} async-done(((bf16[32,1536]{1,0:T(8,128)(2,1)}), bf16[1024,1536]{1,0:T(8,128)(2,1)}) %all-gather.3.cloned.1.call-update) | async-done | bytes 3145744 | tf_op jit(solution)/shard_map/all_gather | solution.py:25
  89.1 9.7 %fusion.8 = f32[1024,1536]{1,0:T(8,128)} fusion(bf16[1024,1536]{1,0:T(8,128)(2,1)} %all-gather.3.cloned.1.call-done, bf16[1536,1536]{1,0:T(8,128)(2,1)} %param.5), kind=kOutput, calls=%fused_computation.13 | convolution fusion | flops 4831838208 | bytes 14155776 | tf_op jit(solution)/shard_map/dot_general | solution.py:30
  98.8 0.0 copy-start.1
  98.8 0.0 copy-start.2
  98.8 0.0 reduce-scatter.3.cloned.1.call-update
  98.9 0.0 all-gather.5.cloned.1.call-start
  98.9 45.2 %reduce-scatter.3.cloned.1.call-done = f32[128,1536]{1,0:T(8,128)} async-done(((f32[1024,1536]{1,0:T(8,128)}), f32[128,1536]{1,0:T(8,128)}) %reduce-scatter.3.cloned.1.call-update) | async-done | bytes 786448 | tf_op jit(solution)/shard_map/reduce_scatter | solution.py:29
  144.1 0.0 copy-done.1
  144.1 0.0 copy-done.2
  144.1 2.6 fusion.7
  146.7 0.0 all-gather.5.cloned.1.call-update
  146.8 0.0 reduce-scatter.5.cloned.1.call-start
  146.8 31.1 %all-gather.5.cloned.1.call-done = bf16[1024,1536]{1,0:T(8,128)(2,1)} async-done(((bf16[128,1536]{1,0:T(8,128)(2,1)}), bf16[1024,1536]{1,0:T(8,128)(2,1)}) %all-gather.5.cloned.1.call-update) | async-done | bytes 3145744 | tf_op jit(solution)/shard_map/all_gather | solution.py:39
  177.9 9.8 %fusion.9 = f32[1024,1536]{1,0:T(8,128)} fusion(bf16[1024,1536]{1,0:T(8,128)(2,1)} %all-gather.5.cloned.1.call-done, bf16[1536,1536]{1,0:T(8,128)(2,1)} %param.5), kind=kOutput, calls=%fused_computation.14 | convolution fusion | flops 4831838208 | bytes 14155776 | tf_op jit(solution)/shard_map/dot_general | solution.py:42
  187.7 0.0 reduce-scatter.5.cloned.1.call-update
  187.7 1.9 copy-done
  189.6 8.7 %fusion = bf16[1536,1536]{0,1:T(8,128)(2,1)} fusion(bf16[1024,1536]{1,0:T(8,128)(2,1)S(1)} %copy-done, bf16[1024,1536]{1,0:T(8,128)(2,1)} %all-gather.3.cloned.1.call-done), kind=kOutput, calls=%fused_computation.1 | convolution fusion | flops 4834197504 | bytes 11010048 | tf_op jit(solution)/shard_map/dot_general | solution.py:49
  198.3 6.6 %copy.8 = bf16[1536,1536]{1,0:T(8,128)(2,1)} copy(bf16[1536,1536]{0,1:T(8,128)(2,1)} %fusion) | data formatting | bytes 9437184
  204.9 1.1 convert_reduce_fusion
  206.0 201.3 %reduce-scatter.5.cloned.1.call-done = f32[32,1536]{1,0:T(8,128)} async-done(((f32[1024,1536]{1,0:T(8,128)}), f32[32,1536]{1,0:T(8,128)}) %reduce-scatter.5.cloned.1.call-update) | async-done | bytes 196624 | tf_op jit(solution)/shard_map/reduce_scatter | solution.py:41
  407.3 1.6 convert_element_type.24
  (1 shorter events, 0.0 us)
Async XLA Ops:
  7.2 82.0 %all-gather.3.cloned.1.call-start = ((), (), s32[]{:S(2)}) async-start(), calls=%async_computation.2 | async-start | bytes 3244032 | tf_op jit(solution)/shard_map/all_gather | solution.py:25
  7.9 136.2 %reduce-scatter.3.cloned.1.call-start = ((), (), s32[]{:S(2)}) async-start(), calls=%async_computation.3 | async-start | bytes 7077888 | tf_op jit(solution)/shard_map/reduce_scatter | solution.py:29
  98.8 45.3 %copy-start.1 = (bf16[128,1536]{1,0:T(8,128)(2,1)S(1)}, bf16[128,1536]{1,0:T(8,128)(2,1)}, u32[]{:S(2)}) copy-start(bf16[128,1536]{1,0:T(8,128)(2,1)} %param.7) | copy-start | bytes 1179652
  98.8 45.3 %copy-start.2 = (f32[1536]{0:T(1024)S(1)}, f32[1536]{0:T(1024)}, u32[]{:S(2)}) copy-start(f32[1536]{0:T(1024)} %param.6) | copy-start | bytes 18436
  98.9 79.0 %all-gather.5.cloned.1.call-start = ((), (), s32[]{:S(2)}) async-start(), calls=%async_computation.4 | async-start | bytes 3538944 | tf_op jit(solution)/shard_map/all_gather | solution.py:39
  146.8 260.6 %reduce-scatter.5.cloned.1.call-start = ((), (), s32[]{:S(2)}) async-start(), calls=%async_computation.5 | async-start | bytes 6488064 | tf_op jit(solution)/shard_map/reduce_scatter | solution.py:41
  187.7 1.9 copy-start
Sparse Core Ops, SparseCore 0:
  10.6 78.5 all-gather.2
  99.0 45.0 reduce-scatter.2
  146.9 30.9 all-gather.4
  187.8 219.4 reduce-scatter.4
where the time goes:
time: 421 us; the launch traced here: 415 us
  waiting for transfers between devices  360 us (86%)
  matrix products  28.2 us (7%)
  between operations  13.8 us (3%)
  local copies, waits for them, and re-layouts  8.49 us (2%)
  other arithmetic  5.26 us (1%)
    reduce_scatter x1, waiting for transfers between devices, body(): lax.psum_scatter(lax.dot_general(block, weight, (((1,), (1,)), ((), ())),...  201 us
    all_gather x1, waiting for transfers between devices, body(): gathered = lax.all_gather(tokens, 'col', axis=0, tiled=True)  81.2 us
    reduce_scatter x1, waiting for transfers between devices, body(): lax.psum_scatter(jnp.dot(block, weight, preferred_element_type=jnp.float3...  45.2 us
    all_gather x1, waiting for transfers between devices, body(): panel = lax.all_gather(slope, 'row', axis=0, tiled=True)  31.1 us
    dot_general x1, matrix products, body(): lax.dot_general(block, weight, (((1,), (1,)), ((), ())), preferred_elemen...  9.77 us
    dot_general x1, matrix products, body(): jnp.dot(block, weight, preferred_element_type=jnp.float32)  9.71 us
    dot_general x1, matrix products, body(): lax.dot_general(gathered, panel, (((0,), (0,)), ((), ())), preferred_elem...  8.7 us
    unnamed x7, local copies, waits for them, and re-layouts  8.49 us
  transfers between devices with their start and end apart: 4, of which 4 were waited for; matrix products, arithmetic and copies ran while one was open for 4% of the time, Pallas kernels for 0%

commit v1 on v0

v1 whole, which is shorter than its diff:
```python
import functools
import math

import jax
import jax.numpy as jnp
from jax import lax
from jax.experimental import pallas as pl
from jax.experimental.pallas import tpu as pltpu
from jax.sharding import PartitionSpec as P

MESH = pl.DeviceIdType.MESH
BF = jnp.bfloat16
F32 = jnp.float32
coeff = math.sqrt(2.0 / math.pi)

OFFS = (0, 1, -1, 2, -2, 3, -3, 4)
SLOT = {d: j for j, d in enumerate(OFFS)}
NG = 8
BLK = 32
GRP = 128
W2 = 768

TICK = 3.93
START = {"A": 10.0, "B": 12.3, "C": 18.0, "D": 24.0, "E": 25.5, "F": 35.0}


def order():
    tasks = []
    for name, start in START.items():
        for j in range(NG):
            tasks.append((start + TICK * j, name, j))
    for s, t in ((1, 14.9), (2, 22.8), (3, 30.7)):
        tasks.append((t, "R", s))
    last = START["E"] + TICK * (NG - 1)
    for n in range(6):
        tasks.append((last + 1.0 + n, "H", n))
    tasks.sort()
    return [(name, j) for _, name, j in tasks]


def body(tokens, weight, bias, gh, o_hid, o_gt, o_gw, o_gb,
         wv, wt, tok, slope, ghv, hidv, own_p, ins, inr, zown, xs, xr, acc, yown, ys, yr, zs, zr, gw, gto,
         y_ss, y_rs, r_ss, r_rs, i_ss, i_rs, x_ss, x_rs, s_ss, s_rs, f_ss, f_rs, b_ss, b_rs, z_ss, z_rs, m_ss, m_rs, l_s):
    row = lax.axis_index("row")
    col = lax.axis_index("col")
    x, k = row // 2, lax.rem(row, 2)
    y, z = col // 8, lax.rem(col, 8)
    other = 1 - k

    def dev(dx=0, dy=0, dz=0, kk=None):
        kk = k if kk is None else kk
        return (lax.rem(x + dx + 4, 4) * 2 + kk, lax.rem(y + dy + 4, 4) * 8 + lax.rem(z + dz + 8, 8))

    mate = dev(kk=other)

    def rcopy(src, dst, ss, rs, to):
        return pltpu.make_async_remote_copy(
            src_ref=src, dst_ref=dst, send_sem=ss, recv_sem=rs, device_id=to, device_id_type=MESH)

    def rows(j, b):
        return pl.ds(pl.multiple_of(j * GRP + b * BLK, BLK), BLK)

    def blk(b):
        return pl.ds(pl.multiple_of(b * BLK, BLK), BLK)

    def ymod(d):
        return lax.rem(y + d + 4, 4)

    def xmod(d):
        return lax.rem(x + d + 4, 4)

    def khalf(h):
        return pl.ds(pl.multiple_of(h * W2, W2), W2)

    sends = []

    def go(cp):
        cp.start()
        sends.append(cp)

    loads = [pltpu.make_async_copy(tokens, tok.at[rows(0, y)], l_s.at[0]),
             pltpu.make_async_copy(weight.at[:, pl.ds(0, W2)], wv.at[0], l_s.at[1]),
             pltpu.make_async_copy(weight.at[:, pl.ds(W2, W2)], wv.at[1], l_s.at[2]),
             pltpu.make_async_copy(gh.at[:, khalf(k)], ghv.at[k], l_s.at[3])]
    for cp in loads:
        cp.start()

    bar = pltpu.get_barrier_semaphore()
    peers = [mate] + [dev(dx=d) for d in (1, 2, 3)] + [dev(dy=d) for d in (1, 2, 3)] + [dev(dz=d) for d in OFFS[1:]]
    for p in peers:
        pl.semaphore_signal(bar, inc=1, device_id=p, device_id_type=MESH)
    pl.semaphore_wait(bar, len(peers))
    loads[0].wait()

    def y_copy(d):
        return rcopy(tok.at[rows(0, y)], tok.at[rows(0, y)], y_ss.at[d - 1], y_rs.at[d - 1], dev(dy=d))

    def y_arrived(d):
        b = ymod(-d)
        rcopy(tok.at[rows(0, b)], tok.at[rows(0, b)], y_ss.at[d - 1], y_rs.at[d - 1], dev(dy=d)).wait_recv()

    def ring_copy(j_from, j_to, i, to):
        b = ymod(-i)
        return rcopy(tok.at[rows(j_from, b)], tok.at[rows(j_to, b)], r_ss.at[j_to, i], r_rs.at[j_to, i], to)

    def ring_send(s, i):
        if s < 3 or i in (0, 1):
            go(ring_copy(SLOT[s], SLOT[s + 1], i, dev(dz=-1)))
        if s < 3 or i in (2, 3):
            go(ring_copy(SLOT[-s], SLOT[-s - 1] if s < 3 else SLOT[4], i, dev(dz=1)))

    def ring_arrived(j, i):
        b = ymod(-i)
        rcopy(tok.at[rows(j, b)], tok.at[rows(j, b)], r_ss.at[j, i], r_rs.at[j, i], mate).wait_recv()

    for d in (1, 3, 2):
        go(y_copy(d))
    ring_send(0, 0)
    ghx = rcopy(gh.at[:, khalf(other)], ghv.at[k], m_ss.at[0], m_rs.at[0], mate)
    go(ghx)

    loads[1].wait()
    loads[2].wait()
    for h in range(2):
        for n in range(0, 1536, 256):
            wt[h, :, n:n + 256] = wv[h, n:n + 256, :].T

    for d in (1, 3, 2):
        y_arrived(d)
        ring_send(0, d)
    loads[3].wait()
    rcopy(gh.at[:, khalf(other)], ghv.at[other], m_ss.at[0], m_rs.at[0], mate).wait_recv()
    o_gb[...] = jnp.zeros_like(o_gb)

    arrived = {0}

    def arrive(j):
        if j in arrived:
            return
        arrived.add(j)
        for i in (0, 1, 3, 2):
            ring_arrived(j, i)

    def do_r(s):
        for i in (0, 1, 3, 2):
            for j in (SLOT[s], SLOT[-s]):
                if j not in arrived:
                    ring_arrived(j, i)
            ring_send(s, i)
        arrived.update((SLOT[s], SLOT[-s]))

    def inner_copy(j):
        return rcopy(ins.at[j], inr.at[j], i_ss.at[j], i_rs.at[j], mate)

    def do_a(j):
        arrive(j)
        t = tok[j * GRP:(j + 1) * GRP, :]
        ins[j] = jnp.dot(t, wv[other], preferred_element_type=F32)
        go(inner_copy(j))
        own_p[j] = jnp.dot(t, wv[k], preferred_element_type=F32)

    def x_copy(j, d):
        return rcopy(xs.at[j, d - 1], xr.at[j, d - 1], x_ss.at[j, d - 1], x_rs.at[j, d - 1], dev(dx=d))

    def do_b(j):
        inner_copy(j).wait_recv()
        for d in (2, 1, 3):
            b = blk(xmod(d))
            xs[j, d - 1] = (own_p[j, b, :] + inr[j, b, :]).astype(BF)
            go(x_copy(j, d))
        b = blk(x)
        zown[j] = own_p[j, b, :] + inr[j, b, :]

    def s_copy(j, i, to, ss, rs, h):
        r = rows(j, xmod(-i))
        return rcopy(slope.at[h, r], slope.at[h, r], ss, rs, to)

    def do_c(j):
        pre = zown[j] + bias[pl.ds(k, 1), :]
        for d in (1, 3, 2):
            x_copy(j, d).wait_recv()
            pre = pre + xr[j, d - 1].astype(F32)
        zb = lax.rem(z + OFFS[j] + 8, 8)
        kr, at = zb // 4, blk(lax.rem(zb, 4))
        sq = pre * pre
        t = jnp.tanh(coeff * (pre + 0.044715 * pre * sq))
        hidv[kr, at, :] = (0.5 * pre * (1.0 + t)).astype(BF)
        dz = 0.5 * (1.0 + t) + 0.5 * pre * (1.0 - t * t) * coeff * (1.0 + 3.0 * 0.044715 * sq)
        slope[k, rows(j, x), :] = (ghv[kr, at, :].astype(F32) * dz).astype(BF)
        for d in (2, 1, 3):
            go(s_copy(j, 0, dev(dx=d), s_ss.at[j, d - 1], s_rs.at[j, d - 1], k))
        go(s_copy(j, 0, mate, f_ss.at[j, 0], f_rs.at[j, 0], k))

    def do_d(j):
        for d in (1, 3, 2):
            s_copy(j, d, mate, s_ss.at[j, d - 1], s_rs.at[j, d - 1], k).wait_recv()
            go(s_copy(j, d, mate, f_ss.at[j, d], f_rs.at[j, d], k))

    def b_copy(j, d):
        return rcopy(ys.at[j, d - 1], yr.at[j, d - 1], b_ss.at[j, d - 1], b_rs.at[j, d - 1], dev(dy=d))

    def do_e(j):
        for i in (0, 1, 3, 2):
            s_copy(j, i, mate, f_ss.at[j, i], f_rs.at[j, i], other).wait_recv()
        g = slice(j * GRP, (j + 1) * GRP)
        acc[...] = (jnp.dot(slope[0, g, :], wt[0], preferred_element_type=F32)
                    + jnp.dot(slope[1, g, :], wt[1], preferred_element_type=F32))
        for d in (2, 1, 3):
            ys[j, d - 1] = acc[blk(ymod(d)), :].astype(BF)
            go(b_copy(j, d))
        yown[j] = acc[blk(y), :]
        for h in range(2):
            o_gb[h:h + 1, :] += jnp.sum(slope[h, g, :].astype(F32), axis=0, keepdims=True)

    def z_copy(j):
        return rcopy(zs.at[j - 1], zr.at[j - 1], z_ss.at[j - 1], z_rs.at[j - 1], dev(dz=OFFS[j]))

    def do_f(j):
        total = yown[j]
        for d in (1, 3, 2):
            b_copy(j, d).wait_recv()
            total = total + yr[j, d - 1].astype(F32)
        if j == 0:
            yown[0] = total
        else:
            zs[j - 1] = total.astype(BF)
            go(z_copy(j))

    outs = []

    def do_h(n):
        cs = slice(n * 256, (n + 1) * 256)
        for h in range(2):
            gw[cs, h * W2:(h + 1) * W2] = lax.dot_general(
                tok[:, cs], slope[h], (((0,), (0,)), ((), ())), preferred_element_type=F32).astype(BF)
        cp = pltpu.make_async_copy(gw.at[cs, :], o_gw.at[cs, :], l_s.at[4 + n])
        cp.start()
        outs.append(cp)

    act = {"A": do_a, "B": do_b, "C": do_c, "D": do_d, "E": do_e, "F": do_f, "R": do_r, "H": do_h}
    done_c = 0
    for name, j in order():
        act[name](j)
        if name == "C":
            done_c += 1
            if done_c == NG:
                go(rcopy(hidv.at[other], o_hid.at[:, khalf(k)], m_ss.at[1], m_rs.at[1], mate))
                cp = pltpu.make_async_copy(hidv.at[k], o_hid.at[:, khalf(k)], l_s.at[10])
                cp.start()
                outs.append(cp)

    total = yown[0]
    for j in range(1, NG):
        z_copy(j).wait_recv()
        total = total + zr[j - 1].astype(F32)
    gto[...] = total.astype(BF)
    cp = pltpu.make_async_copy(gto, o_gt, l_s.at[11])
    cp.start()
    outs.append(cp)
    rcopy(hidv.at[other], o_hid.at[:, khalf(other)], m_ss.at[1], m_rs.at[1], mate).wait_recv()
    for cp in sends:
        cp.wait_send()
    for cp in outs:
        cp.wait()


def local(tokens, weight, bias, gh):
    any_ = pl.BlockSpec(memory_space=pl.ANY)
    vmem = pl.BlockSpec(memory_space=pltpu.VMEM)
    dma = pltpu.SemaphoreType.DMA
    V = pltpu.VMEM
    hid, gt, gw, gb = pl.pallas_call(
        body,
        out_shape=(jax.ShapeDtypeStruct((128, 1536), BF), jax.ShapeDtypeStruct((32, 1536), BF),
                   jax.ShapeDtypeStruct((1536, 1536), BF), jax.ShapeDtypeStruct((2, W2), F32)),
        in_specs=[any_, any_, vmem, any_],
        out_specs=(any_, any_, any_, vmem),
        scratch_shapes=[
            V((2, 1536, W2), BF), V((2, W2, 1536), BF), V((1024, 1536), BF), V((2, 1024, W2), BF),
            V((2, 128, W2), BF), V((2, 128, W2), BF),
            V((NG, GRP, W2), F32), V((NG, GRP, W2), F32), V((NG, GRP, W2), F32), V((NG, BLK, W2), F32),
            V((NG, 3, BLK, W2), BF), V((NG, 3, BLK, W2), BF), V((GRP, 1536), F32), V((NG, BLK, 1536), F32),
            V((NG, 3, BLK, 1536), BF), V((NG, 3, BLK, 1536), BF), V((NG - 1, BLK, 1536), BF), V((NG - 1, BLK, 1536), BF),
            V((1536, 1536), BF), V((BLK, 1536), BF),
            dma((3,)), dma((3,)), dma((NG, 4)), dma((NG, 4)), dma((NG,)), dma((NG,)), dma((NG, 3)), dma((NG, 3)),
            dma((NG, 3)), dma((NG, 3)), dma((NG, 4)), dma((NG, 4)), dma((NG, 3)), dma((NG, 3)),
            dma((NG - 1,)), dma((NG - 1,)), dma((2,)), dma((2,)), dma((12,)),
        ],
        compiler_params=pltpu.CompilerParams(collective_id=0, has_side_effects=True, vmem_limit_bytes=58 * 2**20),
        cost_estimate=pl.CostEstimate(flops=6 * 1024 * 1536 * 1536, bytes_accessed=10 * 2**20, transcendentals=128 * 1536),
        name="layer",
    )(tokens, weight, bias.reshape(2, W2), gh)
    return hid, gt, gw, gb.reshape(1536)


def solution(mesh):
    in_specs = (P("col", "row"), P("row", "col"), P("col"), P("row", "col"))
    out_specs = (P("row", "col"), P("col", "row"), P("row", "col"), P("col"))
    return jax.shard_map(local, mesh=mesh, in_specs=in_specs, out_specs=out_specs, check_vma=False)
```

time: 421 us -> 97.4 us (0.23); the launches traced: 415 us -> 97.1 us
  waiting for transfers between devices: 360 us -> 0 us
  Pallas kernels: 0 us -> 85.8 us
  matrix products: 28.2 us -> 0 us
  between operations: 13.8 us -> 0.64 us
  other arithmetic: 5.26 us -> 0 us
    reduce_scatter x2 -> x0, waiting for transfers between devices: 247 us -> none  [the longest x1 201 us: body(): lax.psum_scatter(lax.dot_general(block, weight, (((1,), (1,)), ((), ())),...]
    all_gather x2 -> x0, waiting for transfers between devices: 112 us -> none  [the longest x1 81.2 us: body(): gathered = lax.all_gather(tokens, 'col', axis=0, tiled=True)]
    pallas_call x0 -> x1, Pallas kernels: none -> 85.8 us  [local(): pl.pallas_call(body, out_shape=(jax.ShapeDtypeStruct((128, 1536), BF), ja...]
    dot_general x3 -> x0, matrix products: 28.2 us -> none  [the longest x1 9.77 us: body(): lax.dot_general(block, weight, (((1,), (1,)), ((), ())), preferred_elemen...]
    unnamed x7 -> x3, local copies, waits for them, and re-layouts: 8.49 us -> 8.13 us
  transfers between devices with their start and end apart: 4 -> 0, of which waited for: 4 -> 0; matrix products, arithmetic and copies ran while one was open for 4% -> 0% of each run, Pallas kernels for 0% -> 0%
where the time goes in v1:
time: 97.4 us; the launch traced here: 97.1 us
  Pallas kernels  85.8 us (88%)
  local copies, waits for them, and re-layouts  10.7 us (11%)
    pallas_call x1, Pallas kernels, local(): pl.pallas_call(body, out_shape=(jax.ShapeDtypeStruct((128, 1536), BF), ja...  85.8 us
    unnamed x3, local copies, waits for them, and re-layouts  8.13 us

profile of v1, /device:TPU:33, one launch (start us, length us, event | category | flops | bytes accessed | tf_op | source)
XLA Modules:
  0.0 97.1 jit_solution(2194121255469488614)
XLA Ops:
  0.6 1.3 %reshape.14.bias = f32[2,768]{1,0:T(2,128)} reshape(f32[1536]{0:T(1024)} %param.6) | data formatting | bytes 12288 | tf_op jit(solution)/shard_map/reshape | solution.py:292
  1.9 85.8 %layer.1 = (bf16[128,1536]{1,0:T(8,128)(2,1)}, bf16[32,1536]{1,0:T(8,128)(2,1)}, bf16[1536,1536]{1,0:T(8,128)(2,1)}, f32[2,768]{1,0:T(2,128)}) custom-call(bf16[32,1536]{1,0:T(8,128)(2,1)} %tokens.1, bf16[1536,1536]{1,0:T(8,128)(2,1)} %weight.1, f32[2,768]{1,0:T(2,128)} %reshape.14.bias, bf16[128,1536]{1,0:T(8,128)(2,1)} %gh.1), custom_call_target="tpu_custom_call" | custom-call | flops 14495514624 | bytes 10485760 | tf_op jit(solution)/shard_map/layer/pallas_call | solution.py:272
  87.7 1.3 %reshape.15 = f32[1536]{0:T(1024)} reshape(f32[2,768]{1,0:T(2,128)} %get-tuple-element.11) | data formatting | bytes 12288 | tf_op jit(solution)/shard_map/reshape | solution.py:293
  89.0 1.8 %copy.11 = bf16[128,1536]{1,0:T(8,128)(2,1)} copy(bf16[128,1536]{1,0:T(8,128)(2,1)} %get-tuple-element.16) | data formatting | bytes 786432
  90.8 1.5 %copy.12 = bf16[32,1536]{1,0:T(8,128)(2,1)} copy(bf16[32,1536]{1,0:T(8,128)(2,1)} %get-tuple-element.17) | data formatting | bytes 196608
  92.3 4.8 %copy.13 = bf16[1536,1536]{1,0:T(8,128)(2,1)} copy(bf16[1536,1536]{1,0:T(8,128)(2,1)} %get-tuple-element.18) | data formatting | bytes 9437184

commit v2 on v0

v2 whole, which is shorter than its diff:
```python
import math

import jax
import jax.numpy as jnp
from jax import lax
from jax.experimental import pallas as pl
from jax.experimental.pallas import tpu as pltpu
from jax.sharding import PartitionSpec as P

MESH = pl.DeviceIdType.MESH
BF = jnp.bfloat16
F32 = jnp.float32
coeff = math.sqrt(2.0 / math.pi)

OFFS = (0, 1, -1, 2, -2, 3, -3, 4)
SLOT = {d: j for j, d in enumerate(OFFS)}
NG = 8
W2 = 768
POS = (0, 1, 3, 2)
MSG = ((0, 1), (1, 3), (3, 4))

ORDER = (
    ("R", 0, 1), ("K", 1), ("A", (0, 0)), ("R", 0, 2), ("R", 1, 0), ("B", (0, 0)), ("A", (0, 1)), ("R", 1, 1),
    ("K", 2), ("R", 1, 2), ("B", (0, 1)), ("A", (1, None)), ("C", (0, 0)), ("A", (2, None)), ("B", (1, None)),
    ("R", 2, 1), ("K", 3), ("B", (2, None)), ("R", 2, 2), ("A", (3, None)), ("D", (0, 0)), ("R", 2, 0), ("C", (0, 1)),
    ("R", 3, 1), ("B", (3, None)), ("K", 4), ("C", (1, None)), ("R", 3, 2), ("A", (4, None)), ("B", (4, None)),
    ("E", (0, 0)), ("C", (3, None)), ("A", (7, None)), ("A", (5, None)), ("D", (1, None)), ("B", (7, None)),
    ("A", (6, None)), ("C", (4, None)), ("E", (1, None)), ("D", (3, None)), ("B", (6, None)), ("E", (3, None)),
    ("C", (7, None)), ("D", (4, None)), ("B", (5, None)), ("R", 3, 0), ("E", (4, None)), ("C", (6, None)),
    ("F", (1, None)), ("C", (2, None)), ("D", (7, None)), ("E", (7, None)), ("C", (5, None)), ("D", (6, None)),
    ("E", (6, None)), ("D", (5, None)), ("D", (2, None)), ("D", (0, 1)), ("F", (3, None)), ("F", (4, None)),
    ("E", (5, None)), ("F", (7, None)), ("E", (2, None)), ("F", (6, None)), ("E", (0, 1)), ("F", (5, None)), ("H", 0),
    ("H", 2), ("F", (2, None)), ("H", 4), ("F", (0, 1)), ("F", (0, 0)),
)


def body(tokens, weight, bias, gh, o_hid, o_gt, o_gw, o_gb,
         wv, wt, tok, slope, ghv, hidv, own_p, ins, inr, zown, xs, xr, acc, yown, ys, yr, zs, zr, bv,
         ss, y_rs, r_rs, k_rs, ky_rs, i_rs, x_rs, s_rs, f_rs, b_rs, m_rs, l_s):
    row = lax.axis_index("row")
    col = lax.axis_index("col")
    x, k = row // 2, lax.rem(row, 2)
    y, z = col // 8, lax.rem(col, 8)
    other = 1 - k

    def dev(dx=0, dy=0, dz=0, kk=None):
        kk = k if kk is None else kk
        return (lax.rem(x + dx + 4, 4) * 2 + kk, lax.rem(y + dy + 4, 4) * 8 + lax.rem(z + dz + 8, 8))

    mate = dev(kk=other)

    def rcopy(src, dst, send, recv, to):
        return pltpu.make_async_remote_copy(
            src_ref=src, dst_ref=dst, send_sem=send, recv_sem=recv, device_id=to, device_id_type=MESH)

    def arrived(dst, recv):
        rcopy(dst, dst, ss.at[0], recv, mate).wait_recv()

    def sent(src, kind):
        rcopy(src, src, ss.at[kind], m_rs.at[0], mate).wait_send()

    def xpos(d):
        i = lax.rem(y - x - d + 8, 4)
        return i + i // 2 - 2 * (i // 3)

    def khalf(h):
        return pl.ds(pl.multiple_of(h * W2, W2), W2)

    def part(ref, it):
        j, h = it
        return ref.at[j] if h is None else ref.at[j, h]

    def block(it, p):
        j, h = it
        return (j, slice(None), p) if h is None else (j, h, p)

    loads = [pltpu.make_async_copy(tokens.at[pl.ds(0, 16)], tok.at[0, 0, 0], l_s.at[0]),
             pltpu.make_async_copy(tokens.at[pl.ds(16, 16)], tok.at[0, 1, 0], l_s.at[1]),
             pltpu.make_async_copy(weight.at[:, pl.ds(0, W2)], wv.at[0], l_s.at[2]),
             pltpu.make_async_copy(weight.at[:, pl.ds(W2, W2)], wv.at[1], l_s.at[3]),
             pltpu.make_async_copy(gh.at[:, khalf(k)], ghv.at[k], l_s.at[4])]
    for cp in loads:
        cp.start()

    bar = pltpu.get_barrier_semaphore()
    peers = [dev(dz=d) for d in (4, 3, -3, 2, -2)] + [dev(dx=d) for d in (2, 1, 3)] + [dev(dy=d) for d in (2, 1, 3)]
    peers += [dev(dz=1), dev(dz=-1), mate]
    for p in peers:
        pl.semaphore_signal(bar, inc=1, device_id=p, device_id_type=MESH)
    pl.semaphore_wait(bar, len(peers))
    loads[0].wait()
    loads[1].wait()

    def ya_send(d):
        rcopy(tok.at[0, 0, 0], tok.at[0, 0, POS[d]], ss.at[0], y_rs.at[d // 2 * (3 - d)], dev(dy=d)).start()

    def ring_send(s, m):
        if s < 3:
            ps = pl.ds(MSG[m][0], MSG[m][1] - MSG[m][0])
            for sign in (1, -1):
                j = SLOT[sign * (s + 1)]
                rcopy(tok.at[SLOT[sign * s], 0, ps], tok.at[j, 0, ps], ss.at[1], r_rs.at[j, m], dev(dz=-sign)).start()
        elif m > 0:
            ps, sign = (pl.ds(0, 2), 1) if m == 1 else (pl.ds(2, 2), -1)
            for q in (m - 1, m):
                ring_wait(SLOT[sign * 3], q)
            rcopy(tok.at[SLOT[sign * 3], 0, ps], tok.at[7, 0, ps], ss.at[1], r_rs.at[7, m], dev(dz=-sign)).start()

    def k_send(s):
        for sign in (1, -1):
            if s < 3:
                j = SLOT[sign * (s + 1)]
                rcopy(tok.at[SLOT[sign * s], 1, 0], tok.at[j, 1, 0], ss.at[2], k_rs.at[j], dev(dz=-sign)).start()
            else:
                cs = pl.ds(0 if sign > 0 else W2, W2)
                rcopy(tok.at[SLOT[sign * s], 1, 0, :, cs], tok.at[7, 1, 0, :, cs], ss.at[2], k_rs.at[7],
                      dev(dz=-sign)).start()

    def ky_send(j):
        for d in (2, 1, 3):
            rcopy(tok.at[j, 1, 0], tok.at[j, 1, POS[d]], ss.at[3], ky_rs.at[j], dev(dy=d)).start()

    for d in (2, 1, 3):
        ya_send(d)
    ring_send(0, 0)
    k_send(0)
    ky_send(0)
    rcopy(gh.at[:, khalf(other)], ghv.at[k], ss.at[10], m_rs.at[0], mate).start()

    loads[2].wait()
    loads[3].wait()

    @pl.loop(0, 6)
    def _(n):
        ns = pl.ds(pl.multiple_of(n * 256, 256), 256)
        for h in range(2):
            wt[h, :, ns] = wv[h, ns, :].T

    bv[0, :] = jnp.where(k == 0, bias[0:W2], bias[W2:2 * W2])
    o_gb[...] = jnp.zeros_like(o_gb)
    loads[4].wait()

    waited = set()

    def ring_wait(j, m):
        if (j, m) in waited:
            return
        waited.add((j, m))
        if j == 0:
            arrived(tok.at[0, 0, pl.ds(1, 2)] if m == 1 else tok.at[0, 0, 3], y_rs.at[m - 1])
        elif j == 7:
            arrived(tok.at[7, 0, pl.ds(0, 2)] if m == 1 else tok.at[7, 0, pl.ds(2, 2)], r_rs.at[7, m])
        else:
            arrived(tok.at[j, 0, pl.ds(MSG[m][0], MSG[m][1] - MSG[m][0])], r_rs.at[j, m])

    def k_wait(j):
        if (j, 3) not in waited:
            waited.add((j, 3))
            arrived(tok.at[j, 1, 0], k_rs.at[j])

    def do_r(s, m):
        for j in {SLOT[s]: 0, SLOT[-s]: 0}:
            ring_wait(j, m)
        ring_send(s, m)

    def do_k(s):
        js = (SLOT[s], SLOT[-s]) if s < 4 else (7,)
        for j in js:
            k_wait(j)
        if s < 4:
            k_send(s)
        for j in js:
            ky_send(j)

    def do_a(it):
        j, h = it
        if h != 1:
            for m in range(3):
                if not (j in (0, 7) and m == 0):
                    ring_wait(j, m)
        if h != 0:
            if j > 0:
                k_wait(j)
            arrived(tok.at[j, 1, pl.ds(1, 3)], ky_rs.at[j])
        t = part(tok, it)[...].reshape(-1, 1536)
        shape = own_p.shape[1:] if h is None else own_p.shape[2:]
        part(ins, it)[...] = jnp.dot(t, wv[other], preferred_element_type=F32).reshape(shape)
        rcopy(part(ins, it), part(inr, it), ss.at[4], i_rs.at[it_at[it]], mate).start()
        part(own_p, it)[...] = jnp.dot(t, wv[k], preferred_element_type=F32).reshape(shape)

    def do_b(it):
        j, h = it
        arrived(part(inr, it), i_rs.at[it_at[it]])
        for d in (2, 1, 3):
            b = block(it, xpos(d))
            at = (j, d - 1) if h is None else (j, d - 1, h)
            xs[at] = (own_p[b] + inr[b]).astype(BF)
            rcopy(xs.at[at], xr.at[at], ss.at[5], x_rs.at[it_at[it]], dev(dx=d)).start()
        b = block(it, xpos(0))
        part(zown, it)[...] = own_p[b] + inr[b]

    def do_c(it):
        j, h = it
        arrived(xr.at[j] if h is None else xr.at[j, :, h], x_rs.at[it_at[it]])
        pre = part(zown, it)[...].reshape(-1, W2) + bv[...]
        for d in (1, 3, 2):
            at = (j, d - 1) if h is None else (j, d - 1, h)
            pre = pre + xr[at].reshape(-1, W2).astype(F32)
        zb = lax.rem(z + OFFS[j] + 8, 8)
        n, off = (32, 0) if h is None else (16, 16 * h)
        kr, rows = zb // 4, pl.ds(pl.multiple_of(lax.rem(zb, 4) * 32 + off, 16), n)
        sq = pre * pre
        t = jnp.tanh(coeff * (pre + 0.044715 * pre * sq))
        dz = 0.5 * (1.0 + t) + 0.5 * pre * (1.0 - t * t) * coeff * (1.0 + 3.0 * 0.044715 * sq)
        s = (ghv[kr, rows, :].astype(F32) * dz).astype(BF)
        b = (k,) + block(it, xpos(0))
        slope[b] = s.reshape((2, 16, W2) if h is None else (16, W2))
        for d in (2, 1, 3):
            rcopy(slope.at[b], slope.at[b], ss.at[6], s_rs.at[it_at[it]], dev(dx=d)).start()
        hidv[kr, rows, :] = (0.5 * pre * (1.0 + t)).astype(BF)

    def do_d(it):
        arrived(slope.at[(k,) + block(it, slice(0, 3))], s_rs.at[it_at[it]])
        mine = part(slope.at[k], it)
        rcopy(mine, mine, ss.at[7], f_rs.at[it_at[it]], mate).start()

    def do_e(it):
        j, h = it
        arrived(part(slope.at[other], it), f_rs.at[it_at[it]])
        s = [part(slope.at[q], it)[...].reshape(-1, W2) for q in range(2)]
        acc[0:s[0].shape[0], :] = (jnp.dot(s[0], wt[0], preferred_element_type=F32)
                                   + jnp.dot(s[1], wt[1], preferred_element_type=F32))
        halves = (0, 1) if h is None else (h,)
        for d in (2, 1, 3):
            for i, q in enumerate(halves):
                r = i * 64 + POS[4 - d] * 16
                ys[j, d - 1, q] = acc[r:r + 16, :].astype(BF)
            at = (j, d - 1) if h is None else (j, d - 1, h)
            rcopy(ys.at[at], yr.at[at], ss.at[8], b_rs.at[it_at[it]], dev(dy=d)).start()
        for i, q in enumerate(halves):
            yown[j, q] = acc[i * 64:i * 64 + 16, :]
        for q in range(2):
            o_gb[q:q + 1, :] += jnp.sum(s[q].astype(F32), axis=0, keepdims=True)

    def do_f(it):
        j, h = it
        arrived(yr.at[j] if h is None else yr.at[j, :, h], b_rs.at[it_at[it]])
        total = part(yown, it)[...]
        for d in (1, 3, 2):
            total = total + yr[(j, d - 1) if h is None else (j, d - 1, h)].astype(F32)
        if j == 0:
            part(yown, it)[...] = total
        else:
            zs[j - 1] = total.astype(BF)
            rcopy(zs.at[j - 1], zr.at[j - 1], ss.at[9], m_rs.at[2], dev(dz=OFFS[j])).start()

    def do_h(first):
        @pl.loop(first, first + 2)
        def _(n):
            cs = pl.ds(pl.multiple_of(n * 256, 256), 256)
            t = tok[:, :, :, :, cs].reshape(1024, 256)
            for h in range(2):
                o_gw[cs, h * W2:(h + 1) * W2] = lax.dot_general(
                    t, slope[h].reshape(1024, W2), (((0,), (0,)), ((), ())), preferred_element_type=F32).astype(BF)

    it_at = {it: n for n, it in enumerate(dict.fromkeys(task[1] for task in ORDER if task[0] == "A"))}
    act = {"A": do_a, "B": do_b, "C": do_c, "D": do_d, "E": do_e, "F": do_f, "R": do_r, "K": do_k, "H": do_h}
    left = len(it_at)
    first_c = True
    for task in ORDER:
        if task[0] == "C" and first_c:
            first_c = False
            arrived(ghv.at[other], m_rs.at[0])
        act[task[0]](*task[1:])
        left -= task[0] == "C"
        if task[0] == "C" and left == 0:
            rcopy(hidv.at[other], o_hid.at[:, khalf(k)], ss.at[11], m_rs.at[1], mate).start()
            o_hid[:, khalf(k)] = hidv[k]

    arrived(o_hid.at[:, khalf(other)], m_rs.at[1])
    sent(tok.at[0, 0, pl.ds(1, 3)], 0)
    sent(tok.at[pl.ds(1, 7), 0], 1)
    sent(tok.at[pl.ds(1, 7), 1, 0], 2)
    sent(tok.at[:, 1, pl.ds(1, 3)], 3)
    sent(ins, 4)
    sent(xs, 5)
    sent(slope.at[0, :, :, pl.ds(0, 3)], 6)
    sent(slope.at[0], 7)
    sent(ys, 8)
    sent(ghv.at[0], 10)
    sent(hidv.at[0], 11)
    total = yown[0]
    arrived(zr, m_rs.at[2])
    for j in range(1, NG):
        total = total + zr[j - 1].astype(F32)
    o_gt[...] = total.reshape(32, 1536).astype(BF)
    sent(zs, 9)


def put(hid, gt, gw, gb, o_hid, o_gt, o_gw, o_gb, sems):
    copies = [pltpu.make_async_copy(src, dst, sems.at[i])
              for i, (src, dst) in enumerate(((gw, o_gw), (hid, o_hid), (gt, o_gt)))]
    for cp in copies:
        cp.start()
    for h in range(2):
        o_gb[h * W2:(h + 1) * W2] = gb[h, :]
    for cp in copies:
        cp.wait()


def local(tokens, weight, bias, gh):
    any_ = pl.BlockSpec(memory_space=pl.ANY)
    vmem = pl.BlockSpec(memory_space=pltpu.VMEM)
    dma = pltpu.SemaphoreType.DMA
    V = pltpu.VMEM
    held = pl.pallas_call(
        body,
        out_shape=(V((128, 1536), BF), V((32, 1536), BF), V((1536, 1536), BF), V((2, W2), F32)),
        in_specs=[any_, any_, vmem, any_],
        out_specs=(vmem,) * 4,
        scratch_shapes=[
            V((2, 1536, W2), BF), V((2, W2, 1536), BF), V((NG, 2, 4, 16, 1536), BF), V((2, NG, 2, 4, 16, W2), BF),
            V((2, 128, W2), BF), V((2, 128, W2), BF),
            V((NG, 2, 4, 16, W2), F32), V((NG, 2, 4, 16, W2), F32), V((NG, 2, 4, 16, W2), F32), V((NG, 2, 16, W2), F32),
            V((NG, 3, 2, 16, W2), BF), V((NG, 3, 2, 16, W2), BF), V((128, 1536), F32), V((NG, 2, 16, 1536), F32),
            V((NG, 3, 2, 16, 1536), BF), V((NG, 3, 2, 16, 1536), BF),
            V((NG - 1, 2, 16, 1536), BF), V((NG - 1, 2, 16, 1536), BF), V((1, W2), F32),
            dma((12,)), dma((2,)), dma((NG, 3)), dma((NG,)), dma((NG,)),
            dma((9,)), dma((9,)), dma((9,)), dma((9,)), dma((9,)), dma((3,)), dma((5,)),
        ],
        compiler_params=pltpu.CompilerParams(collective_id=0, has_side_effects=True, vmem_limit_bytes=58 * 2**20),
        cost_estimate=pl.CostEstimate(flops=6 * 1024 * 1536 * 1536, bytes_accessed=10 * 2**20, transcendentals=128 * 1536),
        name="layer",
    )(tokens, weight, bias, gh)
    held = [pltpu.with_memory_space_constraint(v, pltpu.VMEM) for v in held]
    return pl.pallas_call(
        put,
        out_shape=(jax.ShapeDtypeStruct((128, 1536), BF), jax.ShapeDtypeStruct((32, 1536), BF),
                   jax.ShapeDtypeStruct((1536, 1536), BF), jax.ShapeDtypeStruct((2 * W2,), F32)),
        in_specs=[vmem] * 4,
        out_specs=(any_, any_, any_, vmem),
        scratch_shapes=[dma((3,))],
        compiler_params=pltpu.CompilerParams(vmem_limit_bytes=2 * 2**20),
        name="put",
    )(*held)


def solution(mesh):
    in_specs = (P("col", "row"), P("row", "col"), P("col"), P("row", "col"))
    out_specs = (P("row", "col"), P("col", "row"), P("row", "col"), P("col"))
    return jax.shard_map(local, mesh=mesh, in_specs=in_specs, out_specs=out_specs, check_vma=False)
```

time: 421 us -> 81.7 us (0.19); the launches traced: 415 us -> 81.6 us
  waiting for transfers between devices: 360 us -> 0 us
  Pallas kernels: 0 us -> 80.8 us
  matrix products: 28.2 us -> 0 us
  between operations: 13.8 us -> 0.8 us
  local copies, waits for them, and re-layouts: 8.49 us -> 0 us
  other arithmetic: 5.26 us -> 0 us
    reduce_scatter x2 -> x0, waiting for transfers between devices: 247 us -> none  [the longest x1 201 us: body(): lax.psum_scatter(lax.dot_general(block, weight, (((1,), (1,)), ((), ())),...]
    all_gather x2 -> x0, waiting for transfers between devices: 112 us -> none  [the longest x1 81.2 us: body(): gathered = lax.all_gather(tokens, 'col', axis=0, tiled=True)]
    pallas_call x0 -> x2, Pallas kernels: none -> 80.8 us  [the longest x1 77.9 us: local(): pl.pallas_call(body, out_shape=(V((128, 1536), BF), V((32, 1536), BF), V(...]
    dot_general x3 -> x0, matrix products: 28.2 us -> none  [the longest x1 9.77 us: body(): lax.dot_general(block, weight, (((1,), (1,)), ((), ())), preferred_elemen...]
    unnamed x7 -> x0, local copies, waits for them, and re-layouts: 8.49 us -> none
  transfers between devices with their start and end apart: 4 -> 0, of which waited for: 4 -> 0; matrix products, arithmetic and copies ran while one was open for 4% -> 0% of each run, Pallas kernels for 0% -> 0%
where the time goes in v2:
time: 81.7 us; the launch traced here: 81.6 us
  Pallas kernels  80.8 us (99%)
    pallas_call x1, Pallas kernels, local(): pl.pallas_call(body, out_shape=(V((128, 1536), BF), V((32, 1536), BF), V(...  77.9 us
    pallas_call x1, Pallas kernels, local(): pl.pallas_call(put, out_shape=(jax.ShapeDtypeStruct((128, 1536), BF), jax...  2.93 us

profile of v2, /device:TPU:33, one launch (start us, length us, event | category | flops | bytes accessed | tf_op | source)
XLA Modules:
  0.0 81.6 jit_solution(13688026826309117264)
XLA Ops:
  0.6 77.9 %layer.1 = (bf16[128,1536]{1,0:T(8,128)(2,1)S(1)}, bf16[32,1536]{1,0:T(8,128)(2,1)S(1)}, bf16[1536,1536]{1,0:T(8,128)(2,1)S(1)}, f32[2,768]{1,0:T(2,128)S(1)}) custom-call(bf16[32,1536]{1,0:T(8,128)(2,1)} %tokens.1, bf16[1536,1536]{1,0:T(8,128)(2,1)} %weight.1, f32[1536]{0:T(1024)} %bias.1, bf16[128,1536]{1,0:T(8,128)(2,1)} %gh.1), custom_call_target="tpu_custom_call" | custom-call | flops 14495514624 | bytes 10485760 | tf_op jit(solution)/shard_map/layer/pallas_call | solution.py:316
  78.5 2.9 %put.1 = (bf16[128,1536]{1,0:T(8,128)(2,1)}, bf16[32,1536]{1,0:T(8,128)(2,1)}, bf16[1536,1536]{1,0:T(8,128)(2,1)}, f32[1536]{0:T(1024)}) custom-call(bf16[128,1536]{1,0:T(8,128)(2,1)S(1)} %get-tuple-element.8.hid, bf16[32,1536]{1,0:T(8,128)(2,1)S(1)} %get-tuple-element.9.gt, bf16[1536,1536]{1,0:T(8,128)(2,1)S(1)} %get-tuple-element.10.gw, ...), custom_call_target="tpu_custom_call" | custom-call | tf_op jit(solution)/shard_map/put/pallas_call | solution.py:336

commit v3 on v2

--- a/solution.py
+++ b/solution.py
@@ -20,22 +20,22 @@
 MSG = ((0, 1), (1, 3), (3, 4))
 
 ORDER = (
-    ("R", 0, 1), ("K", 1), ("A", (0, 0)), ("R", 0, 2), ("R", 1, 0), ("B", (0, 0)), ("A", (0, 1)), ("R", 1, 1),
-    ("K", 2), ("R", 1, 2), ("B", (0, 1)), ("A", (1, None)), ("C", (0, 0)), ("A", (2, None)), ("B", (1, None)),
-    ("R", 2, 1), ("K", 3), ("B", (2, None)), ("R", 2, 2), ("A", (3, None)), ("D", (0, 0)), ("R", 2, 0), ("C", (0, 1)),
-    ("R", 3, 1), ("B", (3, None)), ("K", 4), ("C", (1, None)), ("R", 3, 2), ("A", (4, None)), ("B", (4, None)),
-    ("E", (0, 0)), ("C", (3, None)), ("A", (7, None)), ("A", (5, None)), ("D", (1, None)), ("B", (7, None)),
-    ("A", (6, None)), ("C", (4, None)), ("E", (1, None)), ("D", (3, None)), ("B", (6, None)), ("E", (3, None)),
-    ("C", (7, None)), ("D", (4, None)), ("B", (5, None)), ("R", 3, 0), ("E", (4, None)), ("C", (6, None)),
-    ("F", (1, None)), ("C", (2, None)), ("D", (7, None)), ("E", (7, None)), ("C", (5, None)), ("D", (6, None)),
-    ("E", (6, None)), ("D", (5, None)), ("D", (2, None)), ("D", (0, 1)), ("F", (3, None)), ("F", (4, None)),
-    ("E", (5, None)), ("F", (7, None)), ("E", (2, None)), ("F", (6, None)), ("E", (0, 1)), ("F", (5, None)), ("H", 0),
-    ("H", 2), ("F", (2, None)), ("H", 4), ("F", (0, 1)), ("F", (0, 0)),
+    ("R", 0, 1), ("K", 1), ("A", (0, 0)), ("R", 0, 2), ("R", 1, 0), ("B", (0, 0)), ("R", 1, 1), ("K", 2),
+    ("A", (1, None)), ("R", 1, 2), ("R", 2, 0), ("C", (0, 0)), ("B", (1, None)), ("A", (2, None)), ("R", 2, 1),
+    ("K", 3), ("A", (3, None)), ("R", 2, 2), ("B", (2, None)), ("A", (4, None)), ("D", (0, 0)), ("C", (1, None)),
+    ("R", 3, 1), ("B", (4, None)), ("A", (5, None)), ("K", 4), ("R", 3, 2), ("A", (6, None)), ("B", (5, None)),
+    ("D", (1, None)), ("B", (6, None)), ("C", (4, None)), ("A", (7, None)), ("E", (1, None)), ("C", (5, None)),
+    ("R", 3, 0), ("B", (7, None)), ("E", (0, 0)), ("C", (6, None)), ("A", (0, 1)), ("D", (4, None)), ("E", (4, None)),
+    ("B", (3, None)), ("B", (0, 1)), ("D", (5, None)), ("E", (5, None)), ("D", (6, None)), ("C", (7, None)),
+    ("C", (3, None)), ("C", (2, None)), ("C", (0, 1)), ("E", (6, None)), ("F", (4, None)), ("F", (1, None)),
+    ("D", (7, None)), ("E", (7, None)), ("F", (5, None)), ("D", (3, None)), ("E", (3, None)), ("D", (0, 1)),
+    ("D", (2, None)), ("F", (6, None)), ("E", (2, None)), ("F", (0, 0)), ("E", (0, 1)), ("F", (7, None)), ("H", 0),
+    ("F", (3, None)), ("H", 2), ("F", (2, None)), ("F", (0, 1)), ("H", 4),
 )
 
 
 def body(tokens, weight, bias, gh, o_hid, o_gt, o_gw, o_gb,
-         wv, wt, tok, slope, ghv, hidv, own_p, ins, inr, zown, xs, xr, acc, yown, ys, yr, zs, zr, bv,
+         wv, wt, tok, slope, ghv, hidv, own_p, ins, inr, zown, xs, xr, acc, yown, ys, yr, zs, zr, bv, bias1,
          ss, y_rs, r_rs, k_rs, ky_rs, i_rs, x_rs, s_rs, f_rs, b_rs, m_rs, l_s):
     row = lax.axis_index("row")
     col = lax.axis_index("col")
@@ -78,12 +78,13 @@
              pltpu.make_async_copy(tokens.at[pl.ds(16, 16)], tok.at[0, 1, 0], l_s.at[1]),
              pltpu.make_async_copy(weight.at[:, pl.ds(0, W2)], wv.at[0], l_s.at[2]),
              pltpu.make_async_copy(weight.at[:, pl.ds(W2, W2)], wv.at[1], l_s.at[3]),
-             pltpu.make_async_copy(gh.at[:, khalf(k)], ghv.at[k], l_s.at[4])]
+             pltpu.make_async_copy(gh.at[:, khalf(k)], ghv.at[k], l_s.at[4]),
+             pltpu.make_async_copy(bias, bias1, l_s.at[5])]
     for cp in loads:
         cp.start()
 
     bar = pltpu.get_barrier_semaphore()
-    peers = [dev(dz=d) for d in (4, 3, -3, 2, -2)] + [dev(dx=d) for d in (2, 1, 3)] + [dev(dy=d) for d in (2, 1, 3)]
+    peers = [dev(dx=d) for d in (2, 1, 3)] + [dev(dy=d) for d in (2, 1, 3)]
     peers += [dev(dz=1), dev(dz=-1), mate]
     for p in peers:
         pl.semaphore_signal(bar, inc=1, device_id=p, device_id_type=MESH)
@@ -136,7 +137,8 @@
         for h in range(2):
             wt[h, :, ns] = wv[h, ns, :].T
 
-    bv[0, :] = jnp.where(k == 0, bias[0:W2], bias[W2:2 * W2])
+    loads[5].wait()
+    bv[0, :] = jnp.where(k == 0, bias1[0:W2], bias1[W2:2 * W2])
     o_gb[...] = jnp.zeros_like(o_gb)
     loads[4].wait()
 
@@ -297,13 +299,14 @@
     sent(zs, 9)
 
 
-def put(hid, gt, gw, gb, o_hid, o_gt, o_gw, o_gb, sems):
+def put(hid, gt, gw, gb, o_hid, o_gt, o_gw, o_gb, gb1, sems):
     copies = [pltpu.make_async_copy(src, dst, sems.at[i])
-              for i, (src, dst) in enumerate(((gw, o_gw), (hid, o_hid), (gt, o_gt)))]
-    for cp in copies:
+              for i, (src, dst) in enumerate(((gw, o_gw), (hid, o_hid), (gt, o_gt), (gb1, o_gb)))]
+    for cp in copies[:3]:
         cp.start()
     for h in range(2):
-        o_gb[h * W2:(h + 1) * W2] = gb[h, :]
+        gb1[h * W2:(h + 1) * W2] = gb[h, :]
+    copies[3].start()
     for cp in copies:
         cp.wait()
 
@@ -316,7 +319,7 @@
     held = pl.pallas_call(
         body,
         out_shape=(V((128, 1536), BF), V((32, 1536), BF), V((1536, 1536), BF), V((2, W2), F32)),
-        in_specs=[any_, any_, vmem, any_],
+        in_specs=[any_] * 4,
         out_specs=(vmem,) * 4,
         scratch_shapes=[
             V((2, 1536, W2), BF), V((2, W2, 1536), BF), V((NG, 2, 4, 16, 1536), BF), V((2, NG, 2, 4, 16, W2), BF),
@@ -324,9 +327,9 @@
             V((NG, 2, 4, 16, W2), F32), V((NG, 2, 4, 16, W2), F32), V((NG, 2, 4, 16, W2), F32), V((NG, 2, 16, W2), F32),
             V((NG, 3, 2, 16, W2), BF), V((NG, 3, 2, 16, W2), BF), V((128, 1536), F32), V((NG, 2, 16, 1536), F32),
             V((NG, 3, 2, 16, 1536), BF), V((NG, 3, 2, 16, 1536), BF),
-            V((NG - 1, 2, 16, 1536), BF), V((NG - 1, 2, 16, 1536), BF), V((1, W2), F32),
+            V((NG - 1, 2, 16, 1536), BF), V((NG - 1, 2, 16, 1536), BF), V((1, W2), F32), V((2 * W2,), F32),
             dma((12,)), dma((2,)), dma((NG, 3)), dma((NG,)), dma((NG,)),
-            dma((9,)), dma((9,)), dma((9,)), dma((9,)), dma((9,)), dma((3,)), dma((5,)),
+            dma((9,)), dma((9,)), dma((9,)), dma((9,)), dma((9,)), dma((3,)), dma((6,)),
         ],
         compiler_params=pltpu.CompilerParams(collective_id=0, has_side_effects=True, vmem_limit_bytes=58 * 2**20),
         cost_estimate=pl.CostEstimate(flops=6 * 1024 * 1536 * 1536, bytes_accessed=10 * 2**20, transcendentals=128 * 1536),
@@ -338,8 +341,8 @@
         out_shape=(jax.ShapeDtypeStruct((128, 1536), BF), jax.ShapeDtypeStruct((32, 1536), BF),
                    jax.ShapeDtypeStruct((1536, 1536), BF), jax.ShapeDtypeStruct((2 * W2,), F32)),
         in_specs=[vmem] * 4,
-        out_specs=(any_, any_, any_, vmem),
-        scratch_shapes=[dma((3,))],
+        out_specs=(any_,) * 4,
+        scratch_shapes=[V((2 * W2,), F32), dma((4,))],
         compiler_params=pltpu.CompilerParams(vmem_limit_bytes=2 * 2**20),
         name="put",
     )(*held)

time: 81.7 us -> 78.7 us (0.963); the launches traced: 81.6 us -> 77.5 us
  Pallas kernels: 80.8 us -> 76.7 us
    pallas_call x1, Pallas kernels: 77.9 us -> 74.3 us  [local(): pl.pallas_call(body, out_shape=(V((128, 1536), BF), V((32, 1536), BF), V(...]
where the time goes in v3:
time: 78.7 us; the launch traced here: 77.5 us
  Pallas kernels  76.7 us (97%)
  between operations  0.8 us (1%)
    pallas_call x1, Pallas kernels, local(): pl.pallas_call(body, out_shape=(V((128, 1536), BF), V((32, 1536), BF), V(...  74.3 us
    pallas_call x1, Pallas kernels, local(): pl.pallas_call(put, out_shape=(jax.ShapeDtypeStruct((128, 1536), BF), jax...  2.35 us

profile of v3, /device:TPU:33, one launch (start us, length us, event | category | flops | bytes accessed | tf_op | source)
XLA Modules:
  0.0 77.5 jit_solution(10270611520390759281)
XLA Ops:
  0.6 74.3 %layer.1 = (bf16[128,1536]{1,0:T(8,128)(2,1)S(1)}, bf16[32,1536]{1,0:T(8,128)(2,1)S(1)}, bf16[1536,1536]{1,0:T(8,128)(2,1)S(1)}, f32[2,768]{1,0:T(2,128)S(1)}) custom-call(bf16[32,1536]{1,0:T(8,128)(2,1)} %tokens.1, bf16[1536,1536]{1,0:T(8,128)(2,1)} %weight.1, f32[1536]{0:T(1024)} %bias.1, bf16[128,1536]{1,0:T(8,128)(2,1)} %gh.1), custom_call_target="tpu_custom_call" | custom-call | flops 14495514624 | bytes 10485760 | tf_op jit(solution)/shard_map/layer/pallas_call | solution.py:319
  75.0 2.4 %put.1 = (bf16[128,1536]{1,0:T(8,128)(2,1)}, bf16[32,1536]{1,0:T(8,128)(2,1)}, bf16[1536,1536]{1,0:T(8,128)(2,1)}, f32[1536]{0:T(1024)}) custom-call(bf16[128,1536]{1,0:T(8,128)(2,1)S(1)} %get-tuple-element.8.hid, bf16[32,1536]{1,0:T(8,128)(2,1)S(1)} %get-tuple-element.9.gt, bf16[1536,1536]{1,0:T(8,128)(2,1)S(1)} %get-tuple-element.10.gw, ...), custom_call_target="tpu_custom_call" | custom-call | tf_op jit(solution)/shard_map/put/pallas_call | solution.py:339

commit v4 on v3

--- a/solution.py
+++ b/solution.py
@@ -121,10 +121,10 @@
         for d in (2, 1, 3):
             rcopy(tok.at[j, 1, 0], tok.at[j, 1, POS[d]], ss.at[3], ky_rs.at[j], dev(dy=d)).start()
 
+    k_send(0)
     for d in (2, 1, 3):
         ya_send(d)
     ring_send(0, 0)
-    k_send(0)
     ky_send(0)
     rcopy(gh.at[:, khalf(other)], ghv.at[k], ss.at[10], m_rs.at[0], mate).start()
 
@@ -230,15 +230,17 @@
         j, h = it
         arrived(part(slope.at[other], it), f_rs.at[it_at[it]])
         s = [part(slope.at[q], it)[...].reshape(-1, W2) for q in range(2)]
-        acc[0:s[0].shape[0], :] = (jnp.dot(s[0], wt[0], preferred_element_type=F32)
-                                   + jnp.dot(s[1], wt[1], preferred_element_type=F32))
         halves = (0, 1) if h is None else (h,)
-        for d in (2, 1, 3):
-            for i, q in enumerate(halves):
-                r = i * 64 + POS[4 - d] * 16
-                ys[j, d - 1, q] = acc[r:r + 16, :].astype(BF)
-            at = (j, d - 1) if h is None else (j, d - 1, h)
-            rcopy(ys.at[at], yr.at[at], ss.at[8], b_rs.at[it_at[it]], dev(dy=d)).start()
+        for c in range(2):
+            cs = slice(c * W2, (c + 1) * W2)
+            acc[0:s[0].shape[0], cs] = (jnp.dot(s[0], wt[0, :, cs], preferred_element_type=F32)
+                                        + jnp.dot(s[1], wt[1, :, cs], preferred_element_type=F32))
+            for d in (2, 1, 3):
+                for i, q in enumerate(halves):
+                    r = i * 64 + POS[4 - d] * 16
+                    ys[j, d - 1, q, :, cs] = acc[r:r + 16, cs].astype(BF)
+                at = (j, d - 1) + ((slice(None),) if h is None else (h,)) + (slice(None), pl.ds(c * W2, W2))
+                rcopy(ys.at[at], yr.at[at], ss.at[8], b_rs.at[it_at[it]], dev(dy=d)).start()
         for i, q in enumerate(halves):
             yown[j, q] = acc[i * 64:i * 64 + 16, :]
         for q in range(2):

time: 78.7 us -> 78.3 us (level)
  no operation moved by 1% of the time
where the time goes in v4:
time: 78.3 us; the launch traced here: 77.6 us
  Pallas kernels  76.8 us (98%)
  between operations  0.8 us (1%)
    pallas_call x1, Pallas kernels, local(): pl.pallas_call(body, out_shape=(V((128, 1536), BF), V((32, 1536), BF), V(...  74.4 us
    pallas_call x1, Pallas kernels, local(): pl.pallas_call(put, out_shape=(jax.ShapeDtypeStruct((128, 1536), BF), jax...  2.35 us

profile of v4, /device:TPU:33, one launch (start us, length us, event | category | flops | bytes accessed | tf_op | source)
XLA Modules:
  0.0 77.6 jit_solution(4860146432101767887)
XLA Ops:
  0.6 74.4 %layer.1 = (bf16[128,1536]{1,0:T(8,128)(2,1)S(1)}, bf16[32,1536]{1,0:T(8,128)(2,1)S(1)}, bf16[1536,1536]{1,0:T(8,128)(2,1)S(1)}, f32[2,768]{1,0:T(2,128)S(1)}) custom-call(bf16[32,1536]{1,0:T(8,128)(2,1)} %tokens.1, bf16[1536,1536]{1,0:T(8,128)(2,1)} %weight.1, f32[1536]{0:T(1024)} %bias.1, bf16[128,1536]{1,0:T(8,128)(2,1)} %gh.1), custom_call_target="tpu_custom_call" | custom-call | flops 14495514624 | bytes 10485760 | tf_op jit(solution)/shard_map/layer/pallas_call | solution.py:321
  75.1 2.4 %put.1 = (bf16[128,1536]{1,0:T(8,128)(2,1)}, bf16[32,1536]{1,0:T(8,128)(2,1)}, bf16[1536,1536]{1,0:T(8,128)(2,1)}, f32[1536]{0:T(1024)}) custom-call(bf16[128,1536]{1,0:T(8,128)(2,1)S(1)} %get-tuple-element.8.hid, bf16[32,1536]{1,0:T(8,128)(2,1)S(1)} %get-tuple-element.9.gt, bf16[1536,1536]{1,0:T(8,128)(2,1)S(1)} %get-tuple-element.10.gw, ...), custom_call_target="tpu_custom_call" | custom-call | tf_op jit(solution)/shard_map/put/pallas_call | solution.py:341
